TPU v7x, 256 devices: a whole 4x4x8 slice. The times are simulated.
256 devices in a mesh: band: 4 (over y_lo, core), fft: 64 (over x, z, y_hi).
Axes of the slice: x: 4, y: 4 (y_hi: 2, y_lo: 2; y = y_hi * 2 + y_lo), z: 8, core: 2. Of those that a mesh axis runs over, the one named last changes fastest.
Arguments:
- receiving: float32 [16, 128, 128, 128], P('band', 'fft'), may hold values from -6 to 6
- occupied: float32 [4, 128, 128, 128], P('band', 'fft'), may hold values from -6 to 6
- coulomb: float32 [128, 128, 128], P(None, 'fft'), may hold values from 0.06 to 2.5, as said below
- pair_list: int32 [16, 4], P('band'), may hold values 0 or 1
Outputs:
- exchanged: float32 [16, 128, 128, 128], P('band', 'fft')
Inputs may be any that keep to these rules, and one draw needn't show every extreme that they name: coulomb at indices (a, b, c) equals coulomb at ((-a) mod 128, (-b) mod 128, (-c) mod 128).
All inputs are finite; a program needn't handle non-finite values. No bound on the sum of `pair_list` on one device may be relied on, other than what follows from the above.
Results may differ from a plain program's by a relative error of at most 0.00013.
Values sent between devices are 32-bit elements; how exact they have to be, the bound alone decides.
No kernel may reach another device: no remote copies, remote signals or barrier semaphores. Data moves between devices by JAX's collectives and lax.ppermute only.
A program may use at most 64 MiB of HBM per device.

v0:
```python
import math

import jax
import jax.numpy as jnp
from jax import lax
from jax.sharding import PartitionSpec as P

mixing = 0.25
einsum_forms = {1: "bxyz,xk->bkyz", 2: "bxyz,yk->bxkz", 3: "bxyz,zk->bxyk"}


def from_root(block, axis, owner):
    block = jnp.where(lax.axis_index(axis) == owner, block, jnp.zeros_like(block))
    return lax.psum(block, axis)


def tables(length):
    indices = jnp.arange(length, dtype=jnp.int32)
    products = indices[:, None] * indices[None, :] % length
    angles = products.astype(jnp.float32) * (2.0 * math.pi / length)
    return (jnp.cos(angles), jnp.sin(angles))


def transform_axis(operand, matrix, dimension):
    return jnp.einsum(einsum_forms[dimension], operand, matrix, precision=lax.Precision.HIGHEST)


def forward_complex(real_part, imag_part, cos_table, sin_table, dimension):
    new_real = transform_axis(real_part, cos_table, dimension) + transform_axis(
        imag_part, sin_table, dimension
    )
    new_imag = transform_axis(imag_part, cos_table, dimension) - transform_axis(
        real_part, sin_table, dimension
    )
    return (new_real, new_imag)


def inverse_complex(real_part, imag_part, cos_table, sin_table, dimension):
    new_real = transform_axis(real_part, cos_table, dimension) - transform_axis(
        imag_part, sin_table, dimension
    )
    new_imag = transform_axis(imag_part, cos_table, dimension) + transform_axis(
        real_part, sin_table, dimension
    )
    return (new_real, new_imag)


def potentials(density, kernel, cos_table, sin_table):
    real_part = transform_axis(density, cos_table, 3)
    imag_part = -transform_axis(density, sin_table, 3)
    real_part, imag_part = forward_complex(real_part, imag_part, cos_table, sin_table, 2)
    spec_real, spec_imag = forward_complex(
        lax.all_to_all(real_part, "fft", split_axis=2, concat_axis=1, tiled=True),
        lax.all_to_all(imag_part, "fft", split_axis=2, concat_axis=1, tiled=True),
        cos_table,
        sin_table,
        1,
    )
    spec_real = spec_real * kernel
    spec_imag = spec_imag * kernel
    real_part, imag_part = inverse_complex(spec_real, spec_imag, cos_table, sin_table, 1)
    real_part, imag_part = (
        lax.all_to_all(real_part, "fft", split_axis=1, concat_axis=2, tiled=True),
        lax.all_to_all(imag_part, "fft", split_axis=1, concat_axis=2, tiled=True),
    )
    real_part, imag_part = inverse_complex(real_part, imag_part, cos_table, sin_table, 2)
    return transform_axis(real_part, cos_table, 3) - transform_axis(imag_part, sin_table, 3)


def on_device(receiving, occupied, coulomb, pair_list):
    length = receiving.shape[3]
    cos_table, sin_table = tables(length)
    kernel = coulomb * (1.0 / length**3)
    weights = pair_list.astype(jnp.float32)
    per_group = occupied.shape[0]
    orbital_count = per_group * lax.axis_size("band")

    def occupied_step(orbital_index, accumulated):
        source = orbital_index // per_group
        pieces = lax.dynamic_index_in_dim(occupied, orbital_index % per_group, 0, keepdims=False)
        orbital = from_root(pieces, "band", source)
        potential = potentials(receiving * orbital[None], kernel, cos_table, sin_table)
        column = lax.dynamic_index_in_dim(weights, orbital_index, 1, keepdims=False)
        return accumulated + column[:, None, None, None] * orbital[None] * potential

    accumulated = lax.fori_loop(
        0, orbital_count, occupied_step, jnp.zeros(receiving.shape, jnp.float32)
    )
    return -mixing * accumulated


def solution(mesh):
    in_specs = (
        P("band", "fft", None, None),
        P("band", "fft", None, None),
        P(None, "fft", None),
        P("band", None),
    )
    out_specs = P("band", "fft", None, None)
    return jax.shard_map(
        on_device, mesh=mesh, in_specs=in_specs, out_specs=out_specs, check_vma=False
    )
```

profile of v0, /device:TPU:33, one launch (start us, length us, event | category | flops | bytes accessed | tf_op | source)
XLA Modules:
  0.0 682.7 jit_solution(4768139165983037089)
XLA Ops:
  8.4 666.9 %while.17 = (s32[]{:T(128)}, f32[4,2,128,128]{3,2,1,0:T(8,128)S(1)}, f32[4,4]{0,1:T(4,128)S(1)}, f32[1,2,128,128]{3,2,1,0:T(8,128)}, f32[4,2,128,128]{3,2,1,0:T(...) while((s32[]{:T(128)}, ...), condition=%wide.region_2.3_spmd.clone.clone, body=%wide.region_0.2_spmd.clone.clone.sunk | while | flops 4033544192 | bytes 47317396 | solution.py:86
  9.2 46.6 %all-reduce.2.cloned.1.call-done = f32[2,128,128]{2,1,0:T(8,128)} async-done(((f32[2,128,128]{2,1,0:T(8,128)}), f32[2,128,128]{2,1,0:T(8,128)}) %all-reduce.2.cloned.1.call-update) | async-done | bytes 131088 | tf_op jit(solution)/shard_map/while/body/eval_jaxpr/psum | solution.py:14
  55.8 1.8 fusion.275
  61.4 12.1 %all-to-all-start = ((f32[4,2,128,128]{3,1,0,2:T(2,128)}), f32[4,2,128,128]{3,1,0,2:T(2,128)S(1)}, u32[]{:S(2)}, u32[]{:S(2)}) async-start(f32[4,2,128,128]{3,1,0,2:T(2,128)} %copy.86), calls=%async_computation | async-start | bytes 1048576 | tf_op jit(solution)/shard_map/while/body/eval_jaxpr/all_to_all | solution.py:53
  76.4 15.1 %all-to-all-done = f32[4,2,128,128]{3,1,0,2:T(2,128)S(1)} async-done(((f32[4,2,128,128]{3,1,0,2:T(2,128)}), f32[4,2,128,128]{3,1,0,2:T(2,128)S(1)}, u32[]{:S(2)}, u32[]{:S(2)}) %all-to-all-start) | async-done | bytes 524320 | tf_op jit(solution)/shard_map/while/body/eval_jaxpr/all_to_all | solution.py:53
  91.6 6.8 all-to-all-start.1
  98.9 16.9 %all-to-all-done.1 = f32[4,2,128,128]{3,1,0,2:T(2,128)S(1)} async-done(((f32[4,2,128,128]{3,1,0,2:T(2,128)}), f32[4,2,128,128]{3,1,0,2:T(2,128)S(1)}, u32[]{:S(2)}, u32[]{:S(2)}) %all-to-all-start.1) | async-done | bytes 524320 | tf_op jit(solution)/shard_map/while/body/eval_jaxpr/all_to_all | solution.py:54
  118.6 1.1 fusion.284
  119.7 1.1 fusion.281
  123.5 7.1 %all-to-all-start.2 = ((f32[4,128,2,128]{3,2,0,1:T(2,128)}), f32[4,128,2,128]{3,2,0,1:T(2,128)S(1)}, u32[]{:S(2)}, u32[]{:S(2)}) async-start(f32[4,128,2,128]{3,2,0,1:T(2,128)} %copy.92), calls=%async_computation.2 | async-start | bytes 1048576 | tf_op jit(solution)/shard_map/while/body/eval_jaxpr/all_to_all | solution.py:63
  133.3 14.2 %all-to-all-done.2 = f32[4,128,2,128]{3,2,0,1:T(2,128)S(1)} async-done(((f32[4,128,2,128]{3,2,0,1:T(2,128)}), f32[4,128,2,128]{3,2,0,1:T(2,128)S(1)}, u32[]{:S(2)}, u32[]{:S(2)}) %all-to-all-start.2) | async-done | bytes 524320 | tf_op jit(solution)/shard_map/while/body/eval_jaxpr/all_to_all | solution.py:63
  147.5 7.6 %all-to-all-start.3 = ((f32[4,128,2,128]{3,2,0,1:T(2,128)}), f32[4,128,2,128]{3,2,0,1:T(2,128)S(1)}, u32[]{:S(2)}, u32[]{:S(2)}) async-start(f32[4,128,2,128]{3,2,0,1:T(2,128)} %copy.95), calls=%async_computation.3 | async-start | bytes 1048576 | tf_op jit(solution)/shard_map/while/body/eval_jaxpr/all_to_all | solution.py:64
  155.6 16.0 %all-to-all-done.3 = f32[4,128,2,128]{3,2,0,1:T(2,128)S(1)} async-done(((f32[4,128,2,128]{3,2,0,1:T(2,128)}), f32[4,128,2,128]{3,2,0,1:T(2,128)S(1)}, u32[]{:S(2)}, u32[]{:S(2)}) %all-to-all-start.3) | async-done | bytes 524320 | tf_op jit(solution)/shard_map/while/body/eval_jaxpr/all_to_all | solution.py:64
  174.4 1.1 fusion.292
  175.5 1.1 fusion.289
  176.6 1.1 fusion.290
  177.8 1.2 fusion.293
  179.1 1.6 select_bitcast_fusion.2
  180.7 40.7 %all-reduce.2.cloned.1.call-done = f32[2,128,128]{2,1,0:T(8,128)} async-done(((f32[2,128,128]{2,1,0:T(8,128)}), f32[2,128,128]{2,1,0:T(8,128)}) %all-reduce.2.cloned.1.call-update) | async-done | bytes 131088 | tf_op jit(solution)/shard_map/while/body/eval_jaxpr/psum | solution.py:14
  221.3 1.8 fusion.275
  227.0 12.0 %all-to-all-start = ((f32[4,2,128,128]{3,1,0,2:T(2,128)}), f32[4,2,128,128]{3,1,0,2:T(2,128)S(1)}, u32[]{:S(2)}, u32[]{:S(2)}) async-start(f32[4,2,128,128]{3,1,0,2:T(2,128)} %copy.86), calls=%async_computation | async-start | bytes 1048576 | tf_op jit(solution)/shard_map/while/body/eval_jaxpr/all_to_all | solution.py:53
  242.0 15.1 %all-to-all-done = f32[4,2,128,128]{3,1,0,2:T(2,128)S(1)} async-done(((f32[4,2,128,128]{3,1,0,2:T(2,128)}), f32[4,2,128,128]{3,1,0,2:T(2,128)S(1)}, u32[]{:S(2)}, u32[]{:S(2)}) %all-to-all-start) | async-done | bytes 524320 | tf_op jit(solution)/shard_map/while/body/eval_jaxpr/all_to_all | solution.py:53
  257.1 6.8 all-to-all-start.1
  264.5 16.9 %all-to-all-done.1 = f32[4,2,128,128]{3,1,0,2:T(2,128)S(1)} async-done(((f32[4,2,128,128]{3,1,0,2:T(2,128)}), f32[4,2,128,128]{3,1,0,2:T(2,128)S(1)}, u32[]{:S(2)}, u32[]{:S(2)}) %all-to-all-start.1) | async-done | bytes 524320 | tf_op jit(solution)/shard_map/while/body/eval_jaxpr/all_to_all | solution.py:54
  284.1 1.1 fusion.284
  285.3 1.1 fusion.281
  289.1 7.1 %all-to-all-start.2 = ((f32[4,128,2,128]{3,2,0,1:T(2,128)}), f32[4,128,2,128]{3,2,0,1:T(2,128)S(1)}, u32[]{:S(2)}, u32[]{:S(2)}) async-start(f32[4,128,2,128]{3,2,0,1:T(2,128)} %copy.92), calls=%async_computation.2 | async-start | bytes 1048576 | tf_op jit(solution)/shard_map/while/body/eval_jaxpr/all_to_all | solution.py:63
  298.8 14.2 %all-to-all-done.2 = f32[4,128,2,128]{3,2,0,1:T(2,128)S(1)} async-done(((f32[4,128,2,128]{3,2,0,1:T(2,128)}), f32[4,128,2,128]{3,2,0,1:T(2,128)S(1)}, u32[]{:S(2)}, u32[]{:S(2)}) %all-to-all-start.2) | async-done | bytes 524320 | tf_op jit(solution)/shard_map/while/body/eval_jaxpr/all_to_all | solution.py:63
  313.0 7.6 %all-to-all-start.3 = ((f32[4,128,2,128]{3,2,0,1:T(2,128)}), f32[4,128,2,128]{3,2,0,1:T(2,128)S(1)}, u32[]{:S(2)}, u32[]{:S(2)}) async-start(f32[4,128,2,128]{3,2,0,1:T(2,128)} %copy.95), calls=%async_computation.3 | async-start | bytes 1048576 | tf_op jit(solution)/shard_map/while/body/eval_jaxpr/all_to_all | solution.py:64
  321.1 16.0 %all-to-all-done.3 = f32[4,128,2,128]{3,2,0,1:T(2,128)S(1)} async-done(((f32[4,128,2,128]{3,2,0,1:T(2,128)}), f32[4,128,2,128]{3,2,0,1:T(2,128)S(1)}, u32[]{:S(2)}, u32[]{:S(2)}) %all-to-all-start.3) | async-done | bytes 524320 | tf_op jit(solution)/shard_map/while/body/eval_jaxpr/all_to_all | solution.py:64
  339.9 1.1 fusion.292
  341.0 1.1 fusion.289
  342.2 1.1 fusion.290
  343.3 1.2 fusion.293
  345.3 41.6 %all-reduce.2.cloned.1.call-done = f32[2,128,128]{2,1,0:T(8,128)} async-done(((f32[2,128,128]{2,1,0:T(8,128)}), f32[2,128,128]{2,1,0:T(8,128)}) %all-reduce.2.cloned.1.call-update) | async-done | bytes 131088 | tf_op jit(solution)/shard_map/while/body/eval_jaxpr/psum | solution.py:14
  386.9 1.8 fusion.275
  392.5 12.0 %all-to-all-start = ((f32[4,2,128,128]{3,1,0,2:T(2,128)}), f32[4,2,128,128]{3,1,0,2:T(2,128)S(1)}, u32[]{:S(2)}, u32[]{:S(2)}) async-start(f32[4,2,128,128]{3,1,0,2:T(2,128)} %copy.86), calls=%async_computation | async-start | bytes 1048576 | tf_op jit(solution)/shard_map/while/body/eval_jaxpr/all_to_all | solution.py:53
  407.5 15.1 %all-to-all-done = f32[4,2,128,128]{3,1,0,2:T(2,128)S(1)} async-done(((f32[4,2,128,128]{3,1,0,2:T(2,128)}), f32[4,2,128,128]{3,1,0,2:T(2,128)S(1)}, u32[]{:S(2)}, u32[]{:S(2)}) %all-to-all-start) | async-done | bytes 524320 | tf_op jit(solution)/shard_map/while/body/eval_jaxpr/all_to_all | solution.py:53
  422.6 6.8 %all-to-all-start.1 = ((f32[4,2,128,128]{3,1,0,2:T(2,128)}), f32[4,2,128,128]{3,1,0,2:T(2,128)S(1)}, u32[]{:S(2)}, u32[]{:S(2)}) async-start(f32[4,2,128,128]{3,1,0,2:T(2,128)} %copy.89), calls=%async_computation.1 | async-start | bytes 1048576 | tf_op jit(solution)/shard_map/while/body/eval_jaxpr/all_to_all | solution.py:54
  430.0 16.9 %all-to-all-done.1 = f32[4,2,128,128]{3,1,0,2:T(2,128)S(1)} async-done(((f32[4,2,128,128]{3,1,0,2:T(2,128)}), f32[4,2,128,128]{3,1,0,2:T(2,128)S(1)}, u32[]{:S(2)}, u32[]{:S(2)}) %all-to-all-start.1) | async-done | bytes 524320 | tf_op jit(solution)/shard_map/while/body/eval_jaxpr/all_to_all | solution.py:54
  449.7 1.1 fusion.284
  450.8 1.1 fusion.281
  454.6 7.1 %all-to-all-start.2 = ((f32[4,128,2,128]{3,2,0,1:T(2,128)}), f32[4,128,2,128]{3,2,0,1:T(2,128)S(1)}, u32[]{:S(2)}, u32[]{:S(2)}) async-start(f32[4,128,2,128]{3,2,0,1:T(2,128)} %copy.92), calls=%async_computation.2 | async-start | bytes 1048576 | tf_op jit(solution)/shard_map/while/body/eval_jaxpr/all_to_all | solution.py:63
  464.4 14.2 %all-to-all-done.2 = f32[4,128,2,128]{3,2,0,1:T(2,128)S(1)} async-done(((f32[4,128,2,128]{3,2,0,1:T(2,128)}), f32[4,128,2,128]{3,2,0,1:T(2,128)S(1)}, u32[]{:S(2)}, u32[]{:S(2)}) %all-to-all-start.2) | async-done | bytes 524320 | tf_op jit(solution)/shard_map/while/body/eval_jaxpr/all_to_all | solution.py:63
  478.6 7.5 %all-to-all-start.3 = ((f32[4,128,2,128]{3,2,0,1:T(2,128)}), f32[4,128,2,128]{3,2,0,1:T(2,128)S(1)}, u32[]{:S(2)}, u32[]{:S(2)}) async-start(f32[4,128,2,128]{3,2,0,1:T(2,128)} %copy.95), calls=%async_computation.3 | async-start | bytes 1048576 | tf_op jit(solution)/shard_map/while/body/eval_jaxpr/all_to_all | solution.py:64
  486.7 16.0 %all-to-all-done.3 = f32[4,128,2,128]{3,2,0,1:T(2,128)S(1)} async-done(((f32[4,128,2,128]{3,2,0,1:T(2,128)}), f32[4,128,2,128]{3,2,0,1:T(2,128)S(1)}, u32[]{:S(2)}, u32[]{:S(2)}) %all-to-all-start.3) | async-done | bytes 524320 | tf_op jit(solution)/shard_map/while/body/eval_jaxpr/all_to_all | solution.py:64
  507.7 1.1 fusion.290
  508.9 1.2 fusion.293
  510.9 41.2 %all-reduce.2.cloned.1.call-done = f32[2,128,128]{2,1,0:T(8,128)} async-done(((f32[2,128,128]{2,1,0:T(8,128)}), f32[2,128,128]{2,1,0:T(8,128)}) %all-reduce.2.cloned.1.call-update) | async-done | bytes 131088 | tf_op jit(solution)/shard_map/while/body/eval_jaxpr/psum | solution.py:14
  552.1 1.8 fusion.275
  557.7 12.0 %all-to-all-start = ((f32[4,2,128,128]{3,1,0,2:T(2,128)}), f32[4,2,128,128]{3,1,0,2:T(2,128)S(1)}, u32[]{:S(2)}, u32[]{:S(2)}) async-start(f32[4,2,128,128]{3,1,0,2:T(2,128)} %copy.86), calls=%async_computation | async-start | bytes 1048576 | tf_op jit(solution)/shard_map/while/body/eval_jaxpr/all_to_all | solution.py:53
  572.8 15.1 %all-to-all-done = f32[4,2,128,128]{3,1,0,2:T(2,128)S(1)} async-done(((f32[4,2,128,128]{3,1,0,2:T(2,128)}), f32[4,2,128,128]{3,1,0,2:T(2,128)S(1)}, u32[]{:S(2)}, u32[]{:S(2)}) %all-to-all-start) | async-done | bytes 524320 | tf_op jit(solution)/shard_map/while/body/eval_jaxpr/all_to_all | solution.py:53
  587.8 6.8 %all-to-all-start.1 = ((f32[4,2,128,128]{3,1,0,2:T(2,128)}), f32[4,2,128,128]{3,1,0,2:T(2,128)S(1)}, u32[]{:S(2)}, u32[]{:S(2)}) async-start(f32[4,2,128,128]{3,1,0,2:T(2,128)} %copy.89), calls=%async_computation.1 | async-start | bytes 1048576 | tf_op jit(solution)/shard_map/while/body/eval_jaxpr/all_to_all | solution.py:54
  595.2 16.9 %all-to-all-done.1 = f32[4,2,128,128]{3,1,0,2:T(2,128)S(1)} async-done(((f32[4,2,128,128]{3,1,0,2:T(2,128)}), f32[4,2,128,128]{3,1,0,2:T(2,128)S(1)}, u32[]{:S(2)}, u32[]{:S(2)}) %all-to-all-start.1) | async-done | bytes 524320 | tf_op jit(solution)/shard_map/while/body/eval_jaxpr/all_to_all | solution.py:54
  614.9 1.1 fusion.284
  616.0 1.1 fusion.281
  619.8 7.1 %all-to-all-start.2 = ((f32[4,128,2,128]{3,2,0,1:T(2,128)}), f32[4,128,2,128]{3,2,0,1:T(2,128)S(1)}, u32[]{:S(2)}, u32[]{:S(2)}) async-start(f32[4,128,2,128]{3,2,0,1:T(2,128)} %copy.92), calls=%async_computation.2 | async-start | bytes 1048576 | tf_op jit(solution)/shard_map/while/body/eval_jaxpr/all_to_all | solution.py:63
  629.6 14.2 %all-to-all-done.2 = f32[4,128,2,128]{3,2,0,1:T(2,128)S(1)} async-done(((f32[4,128,2,128]{3,2,0,1:T(2,128)}), f32[4,128,2,128]{3,2,0,1:T(2,128)S(1)}, u32[]{:S(2)}, u32[]{:S(2)}) %all-to-all-start.2) | async-done | bytes 524320 | tf_op jit(solution)/shard_map/while/body/eval_jaxpr/all_to_all | solution.py:63
  643.8 7.6 %all-to-all-start.3 = ((f32[4,128,2,128]{3,2,0,1:T(2,128)}), f32[4,128,2,128]{3,2,0,1:T(2,128)S(1)}, u32[]{:S(2)}, u32[]{:S(2)}) async-start(f32[4,128,2,128]{3,2,0,1:T(2,128)} %copy.95), calls=%async_computation.3 | async-start | bytes 1048576 | tf_op jit(solution)/shard_map/while/body/eval_jaxpr/all_to_all | solution.py:64
  651.9 16.0 %all-to-all-done.3 = f32[4,128,2,128]{3,2,0,1:T(2,128)S(1)} async-done(((f32[4,128,2,128]{3,2,0,1:T(2,128)}), f32[4,128,2,128]{3,2,0,1:T(2,128)S(1)}, u32[]{:S(2)}, u32[]{:S(2)}) %all-to-all-start.3) | async-done | bytes 524320 | tf_op jit(solution)/shard_map/while/body/eval_jaxpr/all_to_all | solution.py:64
  670.7 1.1 fusion.292
  671.8 1.1 fusion.289
  672.9 1.1 fusion.290
  674.1 1.2 fusion.293
  (133 shorter events, 81.4 us)
Async XLA Ops:
  6.5 1.9 copy-start
  8.4 47.4 %all-reduce.2.cloned.1.call-start = ((), (), s32[]{:S(2)}) async-start(), calls=%async_computation.4 | async-start | bytes 262144 | tf_op jit(solution)/shard_map/while/body/eval_jaxpr/psum | solution.py:14
  57.6 0.9 copy-start.1
  61.4 30.1 %all-to-all-start = ((f32[4,2,128,128]{3,1,0,2:T(2,128)}), f32[4,2,128,128]{3,1,0,2:T(2,128)S(1)}, u32[]{:S(2)}, u32[]{:S(2)}) async-start(f32[4,2,128,128]{3,1,0,2:T(2,128)} %copy.86), calls=%async_computation | async-start | bytes 1048576 | tf_op jit(solution)/shard_map/while/body/eval_jaxpr/all_to_all | solution.py:53
  91.6 24.2 %all-to-all-start.1 = ((f32[4,2,128,128]{3,1,0,2:T(2,128)}), f32[4,2,128,128]{3,1,0,2:T(2,128)S(1)}, u32[]{:S(2)}, u32[]{:S(2)}) async-start(f32[4,2,128,128]{3,1,0,2:T(2,128)} %copy.89), calls=%async_computation.1 | async-start | bytes 1048576 | tf_op jit(solution)/shard_map/while/body/eval_jaxpr/all_to_all | solution.py:54
  123.5 24.0 %all-to-all-start.2 = ((f32[4,128,2,128]{3,2,0,1:T(2,128)}), f32[4,128,2,128]{3,2,0,1:T(2,128)S(1)}, u32[]{:S(2)}, u32[]{:S(2)}) async-start(f32[4,128,2,128]{3,2,0,1:T(2,128)} %copy.92), calls=%async_computation.2 | async-start | bytes 1048576 | tf_op jit(solution)/shard_map/while/body/eval_jaxpr/all_to_all | solution.py:63
  147.5 24.1 %all-to-all-start.3 = ((f32[4,128,2,128]{3,2,0,1:T(2,128)}), f32[4,128,2,128]{3,2,0,1:T(2,128)S(1)}, u32[]{:S(2)}, u32[]{:S(2)}) async-start(f32[4,128,2,128]{3,2,0,1:T(2,128)} %copy.95), calls=%async_computation.3 | async-start | bytes 1048576 | tf_op jit(solution)/shard_map/while/body/eval_jaxpr/all_to_all | solution.py:64
  179.0 42.3 %all-reduce.2.cloned.1.call-start = ((), (), s32[]{:S(2)}) async-start(), calls=%async_computation.4 | async-start | bytes 262144 | tf_op jit(solution)/shard_map/while/body/eval_jaxpr/psum | solution.py:14
  223.1 0.9 copy-start.1
  227.0 30.1 %all-to-all-start = ((f32[4,2,128,128]{3,1,0,2:T(2,128)}), f32[4,2,128,128]{3,1,0,2:T(2,128)S(1)}, u32[]{:S(2)}, u32[]{:S(2)}) async-start(f32[4,2,128,128]{3,1,0,2:T(2,128)} %copy.86), calls=%async_computation | async-start | bytes 1048576 | tf_op jit(solution)/shard_map/while/body/eval_jaxpr/all_to_all | solution.py:53
  257.1 24.2 %all-to-all-start.1 = ((f32[4,2,128,128]{3,1,0,2:T(2,128)}), f32[4,2,128,128]{3,1,0,2:T(2,128)S(1)}, u32[]{:S(2)}, u32[]{:S(2)}) async-start(f32[4,2,128,128]{3,1,0,2:T(2,128)} %copy.89), calls=%async_computation.1 | async-start | bytes 1048576 | tf_op jit(solution)/shard_map/while/body/eval_jaxpr/all_to_all | solution.py:54
  289.1 24.0 %all-to-all-start.2 = ((f32[4,128,2,128]{3,2,0,1:T(2,128)}), f32[4,128,2,128]{3,2,0,1:T(2,128)S(1)}, u32[]{:S(2)}, u32[]{:S(2)}) async-start(f32[4,128,2,128]{3,2,0,1:T(2,128)} %copy.92), calls=%async_computation.2 | async-start | bytes 1048576 | tf_op jit(solution)/shard_map/while/body/eval_jaxpr/all_to_all | solution.py:63
  313.0 24.1 %all-to-all-start.3 = ((f32[4,128,2,128]{3,2,0,1:T(2,128)}), f32[4,128,2,128]{3,2,0,1:T(2,128)S(1)}, u32[]{:S(2)}, u32[]{:S(2)}) async-start(f32[4,128,2,128]{3,2,0,1:T(2,128)} %copy.95), calls=%async_computation.3 | async-start | bytes 1048576 | tf_op jit(solution)/shard_map/while/body/eval_jaxpr/all_to_all | solution.py:64
  344.6 42.3 %all-reduce.2.cloned.1.call-start = ((), (), s32[]{:S(2)}) async-start(), calls=%async_computation.4 | async-start | bytes 262144 | tf_op jit(solution)/shard_map/while/body/eval_jaxpr/psum | solution.py:14
  388.7 0.9 copy-start.1
  392.5 30.1 %all-to-all-start = ((f32[4,2,128,128]{3,1,0,2:T(2,128)}), f32[4,2,128,128]{3,1,0,2:T(2,128)S(1)}, u32[]{:S(2)}, u32[]{:S(2)}) async-start(f32[4,2,128,128]{3,1,0,2:T(2,128)} %copy.86), calls=%async_computation | async-start | bytes 1048576 | tf_op jit(solution)/shard_map/while/body/eval_jaxpr/all_to_all | solution.py:53
  422.6 24.3 %all-to-all-start.1 = ((f32[4,2,128,128]{3,1,0,2:T(2,128)}), f32[4,2,128,128]{3,1,0,2:T(2,128)S(1)}, u32[]{:S(2)}, u32[]{:S(2)}) async-start(f32[4,2,128,128]{3,1,0,2:T(2,128)} %copy.89), calls=%async_computation.1 | async-start | bytes 1048576 | tf_op jit(solution)/shard_map/while/body/eval_jaxpr/all_to_all | solution.py:54
  454.6 24.0 %all-to-all-start.2 = ((f32[4,128,2,128]{3,2,0,1:T(2,128)}), f32[4,128,2,128]{3,2,0,1:T(2,128)S(1)}, u32[]{:S(2)}, u32[]{:S(2)}) async-start(f32[4,128,2,128]{3,2,0,1:T(2,128)} %copy.92), calls=%async_computation.2 | async-start | bytes 1048576 | tf_op jit(solution)/shard_map/while/body/eval_jaxpr/all_to_all | solution.py:63
  478.6 24.1 %all-to-all-start.3 = ((f32[4,128,2,128]{3,2,0,1:T(2,128)}), f32[4,128,2,128]{3,2,0,1:T(2,128)S(1)}, u32[]{:S(2)}, u32[]{:S(2)}) async-start(f32[4,128,2,128]{3,2,0,1:T(2,128)} %copy.95), calls=%async_computation.3 | async-start | bytes 1048576 | tf_op jit(solution)/shard_map/while/body/eval_jaxpr/all_to_all | solution.py:64
  510.1 42.0 %all-reduce.2.cloned.1.call-start = ((), (), s32[]{:S(2)}) async-start(), calls=%async_computation.4 | async-start | bytes 262144 | tf_op jit(solution)/shard_map/while/body/eval_jaxpr/psum | solution.py:14
  553.9 0.9 copy-start.1
  557.7 30.1 %all-to-all-start = ((f32[4,2,128,128]{3,1,0,2:T(2,128)}), f32[4,2,128,128]{3,1,0,2:T(2,128)S(1)}, u32[]{:S(2)}, u32[]{:S(2)}) async-start(f32[4,2,128,128]{3,1,0,2:T(2,128)} %copy.86), calls=%async_computation | async-start | bytes 1048576 | tf_op jit(solution)/shard_map/while/body/eval_jaxpr/all_to_all | solution.py:53
  587.8 24.3 %all-to-all-start.1 = ((f32[4,2,128,128]{3,1,0,2:T(2,128)}), f32[4,2,128,128]{3,1,0,2:T(2,128)S(1)}, u32[]{:S(2)}, u32[]{:S(2)}) async-start(f32[4,2,128,128]{3,1,0,2:T(2,128)} %copy.89), calls=%async_computation.1 | async-start | bytes 1048576 | tf_op jit(solution)/shard_map/while/body/eval_jaxpr/all_to_all | solution.py:54
  619.8 24.0 %all-to-all-start.2 = ((f32[4,128,2,128]{3,2,0,1:T(2,128)}), f32[4,128,2,128]{3,2,0,1:T(2,128)S(1)}, u32[]{:S(2)}, u32[]{:S(2)}) async-start(f32[4,128,2,128]{3,2,0,1:T(2,128)} %copy.92), calls=%async_computation.2 | async-start | bytes 1048576 | tf_op jit(solution)/shard_map/while/body/eval_jaxpr/all_to_all | solution.py:63
  643.8 24.1 %all-to-all-start.3 = ((f32[4,128,2,128]{3,2,0,1:T(2,128)}), f32[4,128,2,128]{3,2,0,1:T(2,128)S(1)}, u32[]{:S(2)}, u32[]{:S(2)}) async-start(f32[4,128,2,128]{3,2,0,1:T(2,128)} %copy.95), calls=%async_computation.3 | async-start | bytes 1048576 | tf_op jit(solution)/shard_map/while/body/eval_jaxpr/all_to_all | solution.py:64
Sparse Core Ops, SparseCore 0:
  11.9 43.8 all-reduce.1
  182.5 38.8 all-reduce.1
  348.0 38.8 all-reduce.1
  513.3 38.8 all-reduce.1
where the time goes:
time: 687 us; the launch traced here: 683 us
  waiting for transfers between devices  419 us (61%)
  starting transfers between devices  134 us (20%)
  matrix products  84.4 us (12%)
  local copies, waits for them, and re-layouts  26.2 us (4%)
  between operations  13.1 us (2%)
    psum x4, waiting for transfers between devices, from_root(): return lax.psum(block, axis)  170 us
    dot_general x80, matrix products, transform_axis(): jnp.einsum(einsum_forms[dimension], operand, matrix, precision=lax.Precis...  84.4 us
    all_to_all x4, waiting for transfers between devices, potentials(): lax.all_to_all(imag_part, 'fft', split_axis=2, concat_axis=1, tiled=True)  67.6 us
    all_to_all x4, waiting for transfers between devices, potentials(): lax.all_to_all(imag_part, 'fft', split_axis=1, concat_axis=2, tiled=True)  64 us
    all_to_all x4, waiting for transfers between devices, potentials(): lax.all_to_all(real_part, 'fft', split_axis=2, concat_axis=1, tiled=True)  60.4 us
    all_to_all x4, waiting for transfers between devices, potentials(): lax.all_to_all(real_part, 'fft', split_axis=1, concat_axis=2, tiled=True)  56.7 us
    all_to_all x4, starting transfers between devices, potentials(): lax.all_to_all(real_part, 'fft', split_axis=2, concat_axis=1, tiled=True)  48.2 us
    all_to_all x4, starting transfers between devices, potentials(): lax.all_to_all(imag_part, 'fft', split_axis=1, concat_axis=2, tiled=True)  30.2 us
  transfers between devices with their start and end apart: 20, of which 20 were waited for; matrix products, arithmetic and copies ran while one was open for 4% of the time, Pallas kernels for 0%

commit v1 on v0

v1 whole, which is shorter than its diff:
```python
import numpy as np

import jax
import jax.numpy as jnp
from jax import lax
from jax.experimental import pallas as pl
from jax.experimental.pallas import tpu as pltpu
from jax.sharding import PartitionSpec as P

grid = 128
devices = 64
planes = grid // devices
mixing = 0.25


def rotation():
    angles = 2.0 * np.pi / grid * (np.arange(grid)[:, None] * np.arange(grid)[None, :] % grid)
    return np.cos(angles), np.sin(angles)


def halves(matrix):
    high = matrix.astype(jnp.bfloat16)
    low = (matrix - high.astype(np.float64)).astype(jnp.bfloat16)
    return np.stack([high, low])


def tables():
    cos, sin = rotation()
    forward = np.block([[cos, -sin], [sin, cos]])
    inverse = np.block([[cos, sin], [-sin, cos]])
    part, row = np.divmod(np.arange(2 * grid), grid)
    spread = part * grid + row % devices * planes + row // devices
    woven = np.arange(2 * grid) % 2 * grid + np.arange(2 * grid) // 2
    return {
        "z": halves(forward),
        "y": halves(forward.T[spread]),
        "x": halves(forward.T[:, woven]),
        "x_back": halves(inverse.T[woven]),
        "y_back": halves(inverse.T[:, spread]),
        "z_back": halves(inverse),
    }


def split(value):
    high = value.astype(jnp.bfloat16)
    low = (value - high.astype(jnp.float32)).astype(jnp.bfloat16)
    return high, low


def dot(left, right):
    return jnp.dot(left, right, preferred_element_type=jnp.float32)


def right_transform(value, table):
    high, low = split(value)
    return dot(high, table[0]) + (dot(low, table[0]) + dot(high, table[1]))


def left_transform(table, value):
    high, low = split(value)
    return dot(table[0], high) + (dot(table[0], low) + dot(table[1], high))


def stack_parts(value):
    top, bottom = value[:grid], value[grid:]
    return jnp.concatenate(
        [
            jnp.concatenate([top[:, :grid], bottom[:, :grid]], 1),
            jnp.concatenate([top[:, grid:], bottom[:, grid:]], 1),
        ],
        0,
    )


def chunk_row(plane, part, field, fields):
    return ((plane * 2 + part) * fields + field) * planes


def forward_kernel(recv_ref, occ_ref, z_ref, y_ref, out_ref):
    received = recv_ref.shape[0]
    fields = 2 * received
    chunk = planes * 2 * fields * planes
    for plane in range(planes):
        for orbital in range(received):
            density = recv_ref[orbital, plane]
            products = [density * occ_ref[j, plane] for j in range(4)]
            value = jnp.concatenate(
                [
                    jnp.concatenate(products[:2], 1),
                    jnp.concatenate(products[2:], 1),
                ],
                0,
            )
            value = left_transform(y_ref, stack_parts(right_transform(value, z_ref)))
            for part in range(2):
                for field in range(2):
                    start = chunk_row(plane, part, orbital * 2 + field, fields)
                    for place in range(planes):
                        row = part * grid + place * devices
                        out_ref[pl.ds(start + place, devices, stride=chunk), :] = value[
                            row : row + devices, field * grid : (field + 1) * grid
                        ]


def filter_kernel(spec_ref, coulomb_ref, x_ref, back_ref, out_ref):
    columns = spec_ref.shape[0] // (2 * grid)
    for pair in range(columns // (2 * planes)):
        for place in range(planes):
            starts = [(pair * 2 + field) * planes + place for field in range(2)]
            value = jnp.concatenate(
                [spec_ref[pl.ds(start, 2 * grid, stride=columns), :] for start in starts], 1
            )
            kernel = coulomb_ref[:, place, :]
            kernel = jnp.concatenate([kernel, kernel], 1)
            kernel = jnp.concatenate([kernel, kernel], 0)
            value = left_transform(back_ref, left_transform(x_ref, value) * kernel)
            for field, start in enumerate(starts):
                out_ref[pl.ds(start, 2 * grid, stride=columns), :] = value[
                    :, field * grid : (field + 1) * grid
                ]


def inverse_kernel(weights_ref, spec_ref, occ_ref, y_ref, z_ref, out_ref):
    received = out_ref.shape[0]
    fields = 2 * received
    chunk = planes * 2 * fields * planes
    for plane in range(planes):
        for orbital in range(received):
            value = jnp.concatenate(
                [
                    jnp.concatenate(
                        [
                            spec_ref[
                                pl.ds(
                                    chunk_row(plane, part, orbital * 2 + field, fields) + place,
                                    devices,
                                    stride=chunk,
                                ),
                                :,
                            ]
                            for field in range(2)
                        ],
                        1,
                    )
                    for part in range(2)
                    for place in range(planes)
                ],
                0,
            )
            value = right_transform(stack_parts(left_transform(y_ref, value)), z_ref)
            total = jnp.zeros((grid, grid), jnp.float32)
            for j in range(4):
                field, part = divmod(j, 2)
                potential = value[
                    field * grid : (field + 1) * grid, part * grid : (part + 1) * grid
                ]
                total += weights_ref[orbital, j] * occ_ref[j, plane] * potential
            out_ref[orbital, plane] = total


vmem = pl.BlockSpec(memory_space=pltpu.VMEM)
smem = pl.BlockSpec(memory_space=pltpu.SMEM)


def call(kernel, shape, in_specs, *operands):
    return pl.pallas_call(
        kernel,
        out_shape=jax.ShapeDtypeStruct(shape, jnp.float32),
        in_specs=in_specs,
        out_specs=vmem,
        compiler_params=pltpu.CompilerParams(vmem_limit_bytes=40 * 1024 * 1024),
    )(*operands)


def on_device(receiving, occupied, coulomb, pair_list):
    table = tables()
    orbitals = lax.all_gather(occupied, "band", axis=0, tiled=True)
    weights = pair_list.astype(jnp.float32) * (-mixing / grid**3)
    rows = planes * 2 * 2 * receiving.shape[0] * planes
    spectrum = call(
        forward_kernel,
        (devices * rows, grid),
        [vmem] * 4,
        receiving,
        orbitals,
        table["z"],
        table["y"],
    )
    spectrum = lax.all_to_all(
        spectrum.reshape(devices, rows, grid), "fft", split_axis=0, concat_axis=0, tiled=True
    ).reshape(devices * rows, grid)
    spectrum = call(
        filter_kernel,
        spectrum.shape,
        [vmem] * 4,
        spectrum,
        coulomb,
        table["x"],
        table["x_back"],
    )
    spectrum = lax.all_to_all(
        spectrum.reshape(devices, rows, grid), "fft", split_axis=0, concat_axis=0, tiled=True
    ).reshape(devices * rows, grid)
    return call(
        inverse_kernel,
        receiving.shape,
        [smem] + [vmem] * 4,
        weights,
        spectrum,
        orbitals,
        table["y_back"],
        table["z_back"],
    )


def solution(mesh):
    in_specs = (
        P("band", "fft", None, None),
        P("band", "fft", None, None),
        P(None, "fft", None),
        P("band", None),
    )
    out_specs = P("band", "fft", None, None)
    return jax.shard_map(
        on_device, mesh=mesh, in_specs=in_specs, out_specs=out_specs, check_vma=False
    )
```

time: 687 us -> 148 us (0.22)
  waiting for transfers between devices: 419 us -> 50.9 us
  starting transfers between devices: 134 us -> 6.85 us
  matrix products: 84.4 us -> 0 us
  blocking collectives: 0 us -> 73.3 us
  local copies, waits for them, and re-layouts: 26.2 us -> 2.97 us
  between operations: 13.1 us -> 0.07 us
  Pallas kernels: 0 us -> 11.1 us
    all_to_all x16 -> x1, waiting for transfers between devices: 249 us -> 50.9 us  [on_device(): lax.all_to_all(spectrum.reshape(devices, rows, grid), 'fft', split_axis=0...]
    psum x4 -> x0, waiting for transfers between devices: 170 us -> none  [from_root(): return lax.psum(block, axis)]
    all_to_all x16 -> x1, starting transfers between devices: 134 us -> 6.85 us  [on_device(): lax.all_to_all(spectrum.reshape(devices, rows, grid), 'fft', split_axis=0...]
    dot_general x80 -> x0, matrix products: 84.4 us -> none  [transform_axis(): jnp.einsum(einsum_forms[dimension], operand, matrix, precision=lax.Precis...]
    all_to_all x0 -> x1, blocking collectives: none -> 65.4 us  [on_device(): lax.all_to_all(spectrum.reshape(devices, rows, grid), 'fft', split_axis=0...]
    pallas_call x0 -> x3, Pallas kernels: none -> 11.1 us  [call(): pl.pallas_call(kernel, out_shape=jax.ShapeDtypeStruct(shape, jnp.float32)...]
    all_to_all x32 -> x0, local copies, waits for them, and re-layouts: 8.15 us -> none  [the longest x8 2.04 us: potentials(): lax.all_to_all(real_part, 'fft', split_axis=2, concat_axis=1, tiled=True)]
    all_gather x0 -> x1, blocking collectives: none -> 7.97 us  [on_device(): orbitals = lax.all_gather(occupied, 'band', axis=0, tiled=True)]
  transfers between devices with their start and end apart: 20 -> 1, of which waited for: 20 -> 1; matrix products, arithmetic and copies ran while one was open for 4% -> 0% of each run, Pallas kernels for 0% -> 0%
where the time goes in v1:
time: 148 us; the launch traced here: 145 us
  blocking collectives  73.3 us (50%)
  waiting for transfers between devices  50.9 us (34%)
  Pallas kernels  11.1 us (8%)
  starting transfers between devices  6.85 us (5%)
  local copies, waits for them, and re-layouts  2.97 us (2%)
    all_to_all x1, blocking collectives, on_device(): lax.all_to_all(spectrum.reshape(devices, rows, grid), 'fft', split_axis=0...  65.4 us
    all_to_all x1, waiting for transfers between devices, on_device(): lax.all_to_all(spectrum.reshape(devices, rows, grid), 'fft', split_axis=0...  50.9 us
    pallas_call x3, Pallas kernels, call(): pl.pallas_call(kernel, out_shape=jax.ShapeDtypeStruct(shape, jnp.float32)...  11.1 us
    all_gather x1, blocking collectives, on_device(): orbitals = lax.all_gather(occupied, 'band', axis=0, tiled=True)  7.97 us
    all_to_all x1, starting transfers between devices, on_device(): lax.all_to_all(spectrum.reshape(devices, rows, grid), 'fft', split_axis=0...  6.85 us
    unnamed x18, local copies, waits for them, and re-layouts  2.97 us
  transfers between devices with their start and end apart: 1, of which 1 were waited for; matrix products, arithmetic and copies ran while one was open for 0% of the time, Pallas kernels for 0%

profile of v1, /device:TPU:33, one launch (start us, length us, event | category | flops | bytes accessed | tf_op | source)
XLA Modules:
  0.0 145.2 jit_solution(5004383709233076947)
XLA Ops:
  0.0 8.0 %all_gather.3.occ_ref = f32[4,2,128,128]{3,2,1,0:T(8,128)S(1)} all-gather(f32[1,2,128,128]{3,2,1,0:T(8,128)} %param.11), channel_id=1, replica_groups=mesh['band'=4,'fft'=64] {'band'}, dimensions={0}, use_global_device_ids=true | all-gather | bytes 655360 | tf_op jit(solution)/shard_map/all_gather | solution.py:177
  8.0 0.0 copy-start
  8.0 1.0 copy-done
  9.0 0.0 copy-start.1
  9.0 0.9 copy-done.1
  10.0 0.0 copy-start.2
  10.0 0.9 copy-done.2
  10.9 3.0 %shard_map.100 = f32[4096,128]{1,0:T(8,128)S(1)} custom-call(f32[4,2,128,128]{3,2,1,0:T(8,128)S(1)} %copy-done, f32[4,2,128,128]{3,2,1,0:T(8,128)S(1)} %all_gather.3.occ_ref, bf16[2,256,256]{2,1,0:T(8,128)(2,1)S(1)} %copy-done.1, bf16[2,256,256]{2,1,0:T(8,128)(2,1)S(1)} %copy-done.2), custom_call_target="tpu_custom_call" | custom-call | tf_op jit(solution)/shard_map/pallas_call | solution.py:166
  13.9 0.0 copy-start.5
  14.0 0.0 copy-start.6
  14.0 0.0 copy-start.7
  14.0 65.4 %all_to_all.10 = f32[64,64,128]{2,1,0:T(8,128)S(1)} all-to-all(f32[64,64,128]{2,1,0:T(8,128)S(1)} %bitcast.5), channel_id=1, replica_groups=mesh['band'=4,'fft'=64] {'fft'}, dimensions={0} | all-to-all | bytes 4194304 | tf_op jit(solution)/shard_map/all_to_all | solution.py:189
  79.4 0.0 copy-done.5
  79.4 0.0 copy-done.6
  79.4 0.0 copy-done.7
  79.4 4.0 %shard_map.101 = f32[4096,128]{1,0:T(8,128)} custom-call(f32[4096,128]{1,0:T(8,128)S(1)} %bitcast.4, f32[128,2,128]{2,1,0:T(2,128)S(1)} %copy-done.7, bf16[2,256,256]{2,1,0:T(8,128)(2,1)S(1)} %copy-done.5, bf16[2,256,256]{2,1,0:T(8,128)(2,1)S(1)} %copy-done.6), custom_call_target="tpu_custom_call" | custom-call | tf_op jit(solution)/shard_map/pallas_call | solution.py:166
  83.4 0.0 copy-start.8
  83.4 0.0 copy-start.3
  83.4 0.0 copy-start.4
  83.4 6.9 %all-to-all-start.1 = ((f32[64,64,128]{2,1,0:T(8,128)}), f32[64,64,128]{2,1,0:T(8,128)S(1)}, u32[]{:S(2)}, u32[]{:S(2)}) async-start(f32[64,64,128]{2,1,0:T(8,128)} %bitcast.2), calls=%async_computation.1 | async-start | bytes 4194304 | tf_op jit(solution)/shard_map/all_to_all | solution.py:201
  90.2 0.0 copy-done.8
  90.3 50.9 %all-to-all-done.1 = f32[64,64,128]{2,1,0:T(8,128)S(1)} async-done(((f32[64,64,128]{2,1,0:T(8,128)}), f32[64,64,128]{2,1,0:T(8,128)S(1)}, u32[]{:S(2)}, u32[]{:S(2)}) %all-to-all-start.1) | async-done | bytes 2097184 | tf_op jit(solution)/shard_map/all_to_all | solution.py:201
  141.1 0.0 copy-done.3
  141.1 0.0 copy-done.4
  141.1 4.1 %shard_map.102 = f32[4,2,128,128]{3,2,1,0:T(8,128)} custom-call(f32[4,4]{1,0:T(4,128)S(1)} %convert_multiply_fusion.weights_ref, f32[4096,128]{1,0:T(8,128)S(1)} %bitcast.6, f32[4,2,128,128]{3,2,1,0:T(8,128)S(1)} %all_gather.3.occ_ref, bf16[2,256,256]{2,1,0:T(8,128)(2,1)S(1)} %copy-done.3, bf16[2,256,256]{2,1,0:T(8,128)(2,1)S(1)} %copy-done.4), custom_call_target="tpu_custom_call" | custom-call | tf_op jit(solution)/shard_map/pallas_call | solution.py:166
  (1 shorter events, 0.0 us)
Async XLA Ops:
  8.0 1.0 copy-start
  9.0 0.9 copy-start.1
  10.0 0.9 copy-start.2
  13.9 65.4 %copy-start.5 = (bf16[2,256,256]{2,1,0:T(8,128)(2,1)S(1)}, bf16[2,256,256]{2,1,0:T(8,128)(2,1)}, u32[]{:S(2)}) copy-start(bf16[2,256,256]{2,1,0:T(8,128)(2,1)} %constant.16.clone.x_ref) | copy-start | bytes 786436
  14.0 65.4 %copy-start.6 = (bf16[2,256,256]{2,1,0:T(8,128)(2,1)S(1)}, bf16[2,256,256]{2,1,0:T(8,128)(2,1)}, u32[]{:S(2)}) copy-start(bf16[2,256,256]{2,1,0:T(8,128)(2,1)} %constant.17.clone.back_ref) | copy-start | bytes 786436
  14.0 65.4 %copy-start.7 = (f32[128,2,128]{2,1,0:T(2,128)S(1)}, f32[128,2,128]{2,1,0:T(2,128)}, u32[]{:S(2)}) copy-start(f32[128,2,128]{2,1,0:T(2,128)} %coulomb_ref.1) | copy-start | bytes 393220
  83.4 6.9 %copy-start.8 = (s32[4,4]{1,0:T(4,128)S(1)}, s32[4,4]{1,0:T(4,128)}, u32[]{:S(2)}) copy-start(s32[4,4]{1,0:T(4,128)} %param.13) | copy-start | bytes 196
  83.4 57.7 %copy-start.3 = (bf16[2,256,256]{2,1,0:T(8,128)(2,1)S(1)}, bf16[2,256,256]{2,1,0:T(8,128)(2,1)}, u32[]{:S(2)}) copy-start(bf16[2,256,256]{2,1,0:T(8,128)(2,1)} %constant.18.clone.y_ref) | copy-start | bytes 786436
  83.4 57.7 %copy-start.4 = (bf16[2,256,256]{2,1,0:T(8,128)(2,1)S(1)}, bf16[2,256,256]{2,1,0:T(8,128)(2,1)}, u32[]{:S(2)}) copy-start(bf16[2,256,256]{2,1,0:T(8,128)(2,1)} %constant.19.clone.z_ref) | copy-start | bytes 786436
  83.4 57.7 %all-to-all-start.1 = ((f32[64,64,128]{2,1,0:T(8,128)}), f32[64,64,128]{2,1,0:T(8,128)S(1)}, u32[]{:S(2)}, u32[]{:S(2)}) async-start(f32[64,64,128]{2,1,0:T(8,128)} %bitcast.2), calls=%async_computation.1 | async-start | bytes 4194304 | tf_op jit(solution)/shard_map/all_to_all | solution.py:201

commit v2 on v1

v2 whole, which is shorter than its diff:
```python
import functools

import numpy as np

import jax
import jax.numpy as jnp
from jax import lax
from jax.experimental import pallas as pl
from jax.experimental.pallas import tpu as pltpu
from jax.sharding import PartitionSpec as P

grid = 128
mixing = 0.25
slabs = 4
members = 16
run = 2
planes = slabs * run
fields = 2
columns = fields * planes
chunk = planes * 2 * columns
groups = [
    [x * 16 + slab * 4 + rest for x in range(4) for rest in range(4)] for slab in range(slabs)
]


def slab_steps(step):
    return [(index, index ^ (step * 4)) for index in range(64)]


def halves(matrix):
    high = matrix.astype(jnp.bfloat16)
    low = (matrix - high.astype(np.float64)).astype(jnp.bfloat16)
    return np.stack([high, low])


def position(member, plane):
    return member // 4 * 32 + plane // run * 8 + member % 4 * run + plane % run


def tables():
    angles = 2.0 * np.pi / grid * (np.arange(grid)[:, None] * np.arange(grid)[None, :] % grid)
    cos, sin = np.cos(angles), np.sin(angles)
    forward = np.block([[cos, -sin], [sin, cos]])
    inverse = np.block([[cos, sin], [-sin, cos]])
    part, rest = np.divmod(np.arange(2 * grid), grid)
    spread = part * grid + position(rest % members, rest // members)
    rest, part = np.divmod(np.arange(2 * grid), 2)
    woven = part * grid + position(rest // planes, rest % planes)
    return {
        "z": halves(forward),
        "y": halves(forward.T[spread]),
        "x": halves(forward.T[:, woven]),
        "x_back": halves(inverse.T[woven]),
        "y_back": halves(inverse.T[:, spread]),
        "z_back": halves(inverse),
    }


def split(value):
    high = value.astype(jnp.bfloat16)
    low = (value - high.astype(jnp.float32)).astype(jnp.bfloat16)
    return high, low


def dot(left, right):
    return jnp.dot(left, right, preferred_element_type=jnp.float32)


def right_transform(value, table):
    high, low = split(value)
    return dot(high, table[0]) + (dot(low, table[0]) + dot(high, table[1]))


def left_transform(table, value):
    high, low = split(value)
    return dot(table[0], high) + (dot(table[0], low) + dot(table[1], high))


def stack_parts(value):
    top, bottom = value[:grid], value[grid:]
    return jnp.concatenate(
        [
            jnp.concatenate([top[:, :grid], bottom[:, :grid]], 1),
            jnp.concatenate([top[:, grid:], bottom[:, grid:]], 1),
        ],
        0,
    )


def member_rows(plane, part, field, place):
    start = pl.multiple_of(plane * (2 * columns), 2 * columns)
    return pl.ds(start + (part * columns + field * planes + place), members, stride=chunk)


def forward_kernel(slab_ref, r0, r1, r2, r3, occ_ref, z_ref, y_ref, out_ref):
    for step, recv_ref in enumerate((r0, r1, r2, r3)):
        for inner in range(run):
            plane = (slab_ref[0] ^ step) * run + inner
            density = recv_ref[inner]
            products = [density * occ_ref[j, step, inner] for j in range(4)]
            value = jnp.concatenate(
                [
                    jnp.concatenate(products[:2], 1),
                    jnp.concatenate(products[2:], 1),
                ],
                0,
            )
            value = left_transform(y_ref, stack_parts(right_transform(value, z_ref)))
            for part in range(2):
                for field in range(fields):
                    for place in range(planes):
                        row = part * grid + place * members
                        out_ref[member_rows(plane, part, field, place), :] = value[
                            row : row + members, field * grid : (field + 1) * grid
                        ]


def filter_kernel(slab_ref, spec_ref, c0, c1, c2, c3, x_ref, back_ref, out_ref):
    for step, coulomb_ref in enumerate((c0, c1, c2, c3)):
        for inner in range(run):
            place = (slab_ref[0] ^ step) * run + inner
            rows = [
                pl.ds(field * planes + place, 2 * grid, stride=columns)
                for field in range(fields)
            ]
            value = jnp.concatenate([spec_ref[row, :] for row in rows], 1)
            kernel = coulomb_ref[:, inner, :]
            kernel = jnp.concatenate([kernel, kernel], 1)
            kernel = jnp.concatenate([kernel, kernel], 0)
            value = left_transform(back_ref, left_transform(x_ref, value) * kernel)
            for field, row in enumerate(rows):
                out_ref[row, :] = value[:, field * grid : (field + 1) * grid]


def inverse_kernel(slab_ref, weights_ref, spec_ref, occ_ref, y_ref, z_ref, o0, o1, o2, o3):
    slab = slab_ref[0]
    for step, out_ref in enumerate((o0, o1, o2, o3)):
        for inner in range(run):
            plane = (slab ^ step) * run + inner
            value = jnp.concatenate(
                [
                    jnp.concatenate(
                        [
                            spec_ref[member_rows(plane, part, field, place), :]
                            for field in range(fields)
                        ],
                        1,
                    )
                    for part in range(2)
                    for place in range(planes)
                ],
                0,
            )
            value = right_transform(stack_parts(left_transform(y_ref, value)), z_ref)
            total = jnp.zeros((grid, grid), jnp.float32)
            for j in range(4):
                field, part = divmod(j, 2)
                potential = value[
                    field * grid : (field + 1) * grid, part * grid : (part + 1) * grid
                ]
                total += weights_ref[slab, j] * occ_ref[j, step, inner] * potential
            out_ref[inner] = total


def collect_kernel(slab_ref, b0, b1, b2, b3, out_ref):
    for step, block_ref in enumerate((b0, b1, b2, b3)):
        out_ref[slab_ref[0] ^ step] = block_ref[...]


vmem = pl.BlockSpec(memory_space=pltpu.VMEM)
smem = pl.BlockSpec(memory_space=pltpu.SMEM)


def call(kernel, shapes, scalars, *operands):
    shapes = jax.tree.map(
        lambda shape: jax.ShapeDtypeStruct(shape, jnp.float32),
        shapes,
        is_leaf=lambda node: isinstance(node[0], int),
    )
    return pl.pallas_call(
        kernel,
        out_shape=shapes,
        in_specs=[smem] * len(scalars) + [vmem] * len(operands),
        out_specs=jax.tree.map(lambda shape: vmem, shapes),
        compiler_params=pltpu.CompilerParams(vmem_limit_bytes=40 * 1024 * 1024),
    )(*scalars, *operands)


def exchange(block, step):
    if step == 0:
        return block
    return lax.ppermute(block, "fft", slab_steps(step))


def regroup(spectrum):
    return lax.all_to_all(
        spectrum.reshape(members, chunk, grid),
        "fft",
        split_axis=0,
        concat_axis=0,
        axis_index_groups=groups,
        tiled=True,
    ).reshape(spectrum.shape)


def on_device(receiving, occupied, coulomb, pair_list):
    table = tables()
    slab = lax.axis_index("fft") // 4 % slabs
    slab_word = slab.astype(jnp.int32).reshape(1)
    weights = pair_list.astype(jnp.float32) * (-mixing / grid**3)

    orbitals = jnp.concatenate([exchange(occupied, step) for step in range(slabs)], 0)
    orbitals = lax.all_gather(orbitals[None], "band", axis=0, tiled=True)
    received = [
        exchange(lax.dynamic_index_in_dim(receiving, slab ^ step, 0, keepdims=False), step)
        for step in range(slabs)
    ]
    kernels = [exchange(coulomb, step) for step in range(slabs)]

    spectrum = call(
        forward_kernel,
        (members * chunk, grid),
        [slab_word],
        *received,
        orbitals,
        table["z"],
        table["y"],
    )
    spectrum = regroup(spectrum)
    spectrum = call(
        filter_kernel,
        spectrum.shape,
        [slab_word],
        spectrum,
        *kernels,
        table["x"],
        table["x_back"],
    )
    spectrum = regroup(spectrum)
    blocks = call(
        inverse_kernel,
        [(run, grid, grid)] * slabs,
        [slab_word, weights],
        spectrum,
        orbitals,
        table["y_back"],
        table["z_back"],
    )
    blocks = [exchange(block, step) for step, block in enumerate(blocks)]
    return call(collect_kernel, receiving.shape, [slab_word], *blocks)


def solution(mesh):
    in_specs = (
        P("band", "fft", None, None),
        P("band", "fft", None, None),
        P(None, "fft", None),
        P("band", None),
    )
    out_specs = P("band", "fft", None, None)
    return jax.shard_map(
        on_device, mesh=mesh, in_specs=in_specs, out_specs=out_specs, check_vma=False
    )
```

time: 148 us -> 192 us (1.30); the launches traced: 145 us -> 191 us
  blocking collectives: 73.3 us -> 0 us
  waiting for transfers between devices: 50.9 us -> 115 us
  starting transfers between devices: 6.85 us -> 44.5 us
  between operations: 0.07 us -> 13.5 us
  local copies, waits for them, and re-layouts: 2.97 us -> 5.44 us
    ppermute x0 -> x12, waiting for transfers between devices: none -> 67.7 us  [exchange(): return lax.ppermute(block, 'fft', slab_steps(step))]
    all_to_all x1 -> x0, blocking collectives: 65.4 us -> none  [on_device(): lax.all_to_all(spectrum.reshape(devices, rows, grid), 'fft', split_axis=0...]
    ppermute x0 -> x12, starting transfers between devices: none -> 24.4 us  [exchange(): return lax.ppermute(block, 'fft', slab_steps(step))]
    all_to_all x1 -> x2, waiting for transfers between devices: 50.9 us -> 34.1 us  [regroup(): lax.all_to_all(spectrum.reshape(members, chunk, grid), 'fft', split_axis=...]
    all_gather x0 -> x1, waiting for transfers between devices: none -> 13.5 us  [on_device(): orbitals = lax.all_gather(orbitals[None], 'band', axis=0, tiled=True)]
    all_to_all x1 -> x2, starting transfers between devices: 6.85 us -> 20 us  [regroup(): lax.all_to_all(spectrum.reshape(members, chunk, grid), 'fft', split_axis=...]
    all_gather x1 -> x0, blocking collectives: 7.97 us -> none  [on_device(): orbitals = lax.all_gather(occupied, 'band', axis=0, tiled=True)]
    unnamed x18 -> x24, local copies, waits for them, and re-layouts: 2.97 us -> 4.3 us
  transfers between devices with their start and end apart: 1 -> 15, of which waited for: 1 -> 10; matrix products, arithmetic and copies ran while one was open for 0% -> 1% of each run, Pallas kernels for 0% -> 0%
where the time goes in v2:
time: 192 us; the launch traced here: 191 us
  waiting for transfers between devices  115 us (60%)
  starting transfers between devices  44.5 us (23%)
  between operations  13.5 us (7%)
  Pallas kernels  10.9 us (6%)
  local copies, waits for them, and re-layouts  5.44 us (3%)
    ppermute x12, waiting for transfers between devices, exchange(): return lax.ppermute(block, 'fft', slab_steps(step))  67.7 us
    all_to_all x2, waiting for transfers between devices, regroup(): lax.all_to_all(spectrum.reshape(members, chunk, grid), 'fft', split_axis=...  34.1 us
    ppermute x12, starting transfers between devices, exchange(): return lax.ppermute(block, 'fft', slab_steps(step))  24.4 us
    all_to_all x2, starting transfers between devices, regroup(): lax.all_to_all(spectrum.reshape(members, chunk, grid), 'fft', split_axis=...  20 us
    all_gather x1, waiting for transfers between devices, on_device(): orbitals = lax.all_gather(orbitals[None], 'band', axis=0, tiled=True)  13.5 us
    pallas_call x4, Pallas kernels, call(): pl.pallas_call(kernel, out_shape=shapes, in_specs=[smem] * len(scalars) +...  10.9 us
    unnamed x24, local copies, waits for them, and re-layouts  4.3 us
  transfers between devices with their start and end apart: 15, of which 10 were waited for; matrix products, arithmetic and copies ran while one was open for 1% of the time, Pallas kernels for 0%

profile of v2, /device:TPU:33, one launch (start us, length us, event | category | flops | bytes accessed | tf_op | source)
XLA Modules:
  0.0 191.5 jit_solution(11343334218579054601)
XLA Ops:
  6.5 0.0 copy-start.8
  6.5 0.0 copy-start.9
  6.5 0.0 all-gather.3.cloned.1.call-start
  6.5 3.0 %collective-permute-start.3 = (f32[1,2,128,128]{3,2,1,0:T(8,128)}, f32[1,2,128,128]{3,2,1,0:T(8,128)S(1)}, u32[]{:S(2)}, u32[]{:S(2)}) collective-permute-start(f32[1,2,128,128]{3,2,1,0:T(8,128)} %param.11), channel_id=1, source_target_pairs={{0,4},{1,5},{2,6},{3,7},{4,0},{5,1},{6,2},{7,3},{8,12},{9,13},{10,... | collective-permute-start | bytes 393224 | tf_op jit(solution)/shard_map/ppermute | solution.py:192
  9.5 4.2 %collective-permute-start.4 = (f32[1,2,128,128]{3,2,1,0:T(8,128)}, f32[1,2,128,128]{3,2,1,0:T(8,128)S(1)}, u32[]{:S(2)}, u32[]{:S(2)}) collective-permute-start(f32[1,2,128,128]{3,2,1,0:T(8,128)} %param.11), channel_id=1, source_target_pairs={{0,8},{1,9},{2,10},{3,11},{4,12},{5,13},{6,14},{7,15},{8,0},{9,1},... | collective-permute-start | bytes 393224 | tf_op jit(solution)/shard_map/ppermute | solution.py:192
  13.7 0.0 collective-permute-start.5
  13.7 6.4 %collective-permute-done.3 = f32[1,2,128,128]{3,2,1,0:T(8,128)S(1)} collective-permute-done((f32[1,2,128,128]{3,2,1,0:T(8,128)}, f32[1,2,128,128]{3,2,1,0:T(8,128)S(1)}, u32[]{:S(2)}, u32[]{:S(2)}) %collective-permute-start.3) | collective-permute-done | bytes 131104 | tf_op jit(solution)/shard_map/ppermute | solution.py:192
  20.1 0.0 collective-permute-done.4
  20.1 5.6 %collective-permute-done.5 = f32[1,2,128,128]{3,2,1,0:T(8,128)S(1)} collective-permute-done((f32[1,2,128,128]{3,2,1,0:T(8,128)}, f32[1,2,128,128]{3,2,1,0:T(8,128)S(1)}, u32[]{:S(2)}, u32[]{:S(2)}) %collective-permute-start.5) | collective-permute-done | bytes 131104 | tf_op jit(solution)/shard_map/ppermute | solution.py:192
  25.8 1.7 pad_maximum_fusion
  27.5 0.0 all-gather.3.cloned.1.call-update
  27.6 1.1 dynamic-slice_bitcast_fusion
  28.7 0.7 collective-permute-start
  29.5 4.2 %collective-permute-start.1 = (f32[2,128,128]{2,1,0:T(8,128)S(1)}, f32[2,128,128]{2,1,0:T(8,128)S(1)}, u32[]{:S(2)}, u32[]{:S(2)}) collective-permute-start(f32[2,128,128]{2,1,0:T(8,128)S(1)} %get-tuple-element.16), channel_id=1, source_target_pairs={{0,8},{1,9},{2,10},{3,11},{4,12},{5,13},{6,14},{7,15},{8,0},{9,1},... | collective-permute-start | bytes 393224 | tf_op jit(solution)/shard_map/ppermute | solution.py:192
  33.6 0.8 collective-permute-start.2
  34.5 0.0 collective-permute-done.r1
  34.5 4.4 %collective-permute-done.1.r2 = f32[2,128,128]{2,1,0:T(8,128)S(1)} collective-permute-done((f32[2,128,128]{2,1,0:T(8,128)S(1)}, f32[2,128,128]{2,1,0:T(8,128)S(1)}, u32[]{:S(2)}, u32[]{:S(2)}) %collective-permute-start.1) | collective-permute-done | bytes 131104 | tf_op jit(solution)/shard_map/ppermute | solution.py:192
  38.8 8.7 %collective-permute-done.2.r3 = f32[2,128,128]{2,1,0:T(8,128)S(1)} collective-permute-done((f32[2,128,128]{2,1,0:T(8,128)S(1)}, f32[2,128,128]{2,1,0:T(8,128)S(1)}, u32[]{:S(2)}, u32[]{:S(2)}) %collective-permute-start.2) | collective-permute-done | bytes 131104 | tf_op jit(solution)/shard_map/ppermute | solution.py:192
  47.5 13.5 %all-gather.3.cloned.1.call-done = f32[16,2,128,128]{3,2,1,0:T(8,128)} async-done(((f32[4,2,128,128]{3,2,1,0:T(8,128)}), f32[16,2,128,128]{3,2,1,0:T(8,128)}) %all-gather.3.cloned.1.call-update) | async-done | bytes 2097168 | tf_op jit(solution)/shard_map/all_gather | solution.py:213
  61.1 0.0 copy-done.8
  61.1 0.0 copy-done.9
  61.1 0.0 copy-start
  61.1 1.6 copy-done
  62.7 3.0 %shard_map.100 = f32[4096,128]{1,0:T(8,128)S(1)} custom-call(s32[1]{0:T(128)} %bitcast.slab_ref, f32[2,128,128]{2,1,0:T(8,128)S(1)} %get-tuple-element.15.r0, f32[2,128,128]{2,1,0:T(8,128)S(1)} %collective-permute-done.r1, f32[2,128,128]{2,1,0:T(8,128)S(1)} %collective-permute-done.1.r2, f32[2,128,128]{2,1,0:T(8,128)S(1)} %collective-permute-done.2.r3, ...), custom_call_target="tpu_custom_call" | custom-call | tf_op jit(solution)/shard_map/pallas_call | solution.py:180
  65.7 0.0 copy-start.2
  65.7 1.3 copy-done.2
  67.0 0.0 copy-start.10
  67.0 0.0 copy-start.6
  67.0 0.0 copy-start.7
  67.0 7.5 %all-to-all-start = ((f32[16,256,128]{2,1,0:T(8,128)}), f32[16,256,128]{2,1,0:T(8,128)S(1)}, u32[]{:S(2)}, u32[]{:S(2)}) async-start(f32[16,256,128]{2,1,0:T(8,128)} %bitcast.17), calls=%async_computation | async-start | bytes 4194304 | tf_op jit(solution)/shard_map/all_to_all | solution.py:196
  74.5 0.0 copy-done.10
  74.5 2.3 %collective-permute-start.6 = (f32[128,2,128]{2,1,0:T(2,128)S(1)}, f32[128,2,128]{2,1,0:T(2,128)S(1)}, u32[]{:S(2)}, u32[]{:S(2)}) collective-permute-start(f32[128,2,128]{2,1,0:T(2,128)S(1)} %copy-done.10), channel_id=1, source_target_pairs={{0,4},{1,5},{2,6},{3,7},{4,0},{5,1},{6,2},{7,3},{8,12},{9,13},{10,... | collective-permute-start | bytes 393224 | tf_op jit(solution)/shard_map/ppermute | solution.py:192
  76.8 2.8 %collective-permute-start.7 = (f32[128,2,128]{2,1,0:T(2,128)S(1)}, f32[128,2,128]{2,1,0:T(2,128)S(1)}, u32[]{:S(2)}, u32[]{:S(2)}) collective-permute-start(f32[128,2,128]{2,1,0:T(2,128)S(1)} %copy-done.10), channel_id=1, source_target_pairs={{0,8},{1,9},{2,10},{3,11},{4,12},{5,13},{6,14},{7,15},{8,0},{9,1},... | collective-permute-start | bytes 393224 | tf_op jit(solution)/shard_map/ppermute | solution.py:192
  79.6 0.6 collective-permute-start.8
  80.2 31.9 %collective-permute-done.6.c1 = f32[128,2,128]{2,1,0:T(2,128)S(1)} collective-permute-done((f32[128,2,128]{2,1,0:T(2,128)S(1)}, f32[128,2,128]{2,1,0:T(2,128)S(1)}, u32[]{:S(2)}, u32[]{:S(2)}) %collective-permute-start.6) | collective-permute-done | bytes 131104 | tf_op jit(solution)/shard_map/ppermute | solution.py:192
  112.2 1.7 collective-permute-done.7.c2
  113.9 0.0 collective-permute-done.8.c3
  113.9 0.0 all-to-all-done
  113.9 0.0 copy-done.6
  113.9 0.0 copy-done.7
  113.9 2.7 %shard_map.101 = f32[4096,128]{1,0:T(8,128)S(1)} custom-call(s32[1]{0:T(128)} %bitcast.slab_ref, f32[4096,128]{1,0:T(8,128)S(1)} %bitcast.16, f32[128,2,128]{2,1,0:T(2,128)S(1)} %copy-done.10, f32[128,2,128]{2,1,0:T(2,128)S(1)} %collective-permute-done.6.c1, f32[128,2,128]{2,1,0:T(2,128)S(1)} %collective-permute-done.7.c2, ...), custom_call_target="tpu_custom_call" | custom-call | tf_op jit(solution)/shard_map/pallas_call | solution.py:180
  116.6 0.0 copy-start.3
  116.6 1.4 copy-done.3
  118.0 0.0 copy-start.11
  118.0 0.0 copy-start.1
  118.0 0.0 copy-start.4
  118.0 0.0 copy-start.5
  118.0 12.6 %all-to-all-start.1 = ((f32[16,256,128]{2,1,0:T(8,128)}), f32[16,256,128]{2,1,0:T(8,128)}, u32[]{:S(2)}, u32[]{:S(2)}) async-start(f32[16,256,128]{2,1,0:T(8,128)} %bitcast.18), calls=%async_computation.1 | async-start | bytes 4194304 | tf_op jit(solution)/shard_map/all_to_all | solution.py:196
  130.6 0.0 copy-done.11
  130.6 34.1 %all-to-all-done.1 = f32[16,256,128]{2,1,0:T(8,128)} async-done(((f32[16,256,128]{2,1,0:T(8,128)}), f32[16,256,128]{2,1,0:T(8,128)}, u32[]{:S(2)}, u32[]{:S(2)}) %all-to-all-start.1) | async-done | bytes 2097184 | tf_op jit(solution)/shard_map/all_to_all | solution.py:196
  164.7 0.0 copy-done.1
  164.7 0.0 copy-done.4
  164.7 0.0 copy-done.5
  164.7 4.3 %shard_map.102 = (f32[2,128,128]{2,1,0:T(8,128)S(1)}, f32[2,128,128]{2,1,0:T(8,128)S(1)}, f32[2,128,128]{2,1,0:T(8,128)S(1)}, f32[2,128,128]{2,1,0:T(8,128)S(1)}) custom-call(s32[1]{0:T(128)} %bitcast.slab_ref, f32[4,4]{1,0:T(4,128)S(1)} %convert_multiply_fusion.weights_ref, f32[4096,128]{1,0:T(8,128)} %bitcast.9.spec_ref, ...), custom_call_target="tpu_custom_call" | custom-call | tf_op jit(solution)/shard_map/pallas_call | solution.py:180
  169.0 1.4 collective-permute-start.10
  170.4 1.5 collective-permute-start.11
  171.9 2.9 %collective-permute-start.9 = (f32[2,128,128]{2,1,0:T(8,128)S(1)}, f32[2,128,128]{2,1,0:T(8,128)S(1)}, u32[]{:S(2)}, u32[]{:S(2)}) collective-permute-start(f32[2,128,128]{2,1,0:T(8,128)S(1)} %get-tuple-element.10), channel_id=1, source_target_pairs={{0,4},{1,5},{2,6},{3,7},{4,0},{5,1},{6,2},{7,3},{8,12},{9,13},{10,... | collective-permute-start | bytes 393224 | tf_op jit(solution)/shard_map/ppermute | solution.py:192
  174.8 8.0 %collective-permute-done.10.b2 = f32[2,128,128]{2,1,0:T(8,128)S(1)} collective-permute-done((f32[2,128,128]{2,1,0:T(8,128)S(1)}, f32[2,128,128]{2,1,0:T(8,128)S(1)}, u32[]{:S(2)}, u32[]{:S(2)}) %collective-permute-start.10) | collective-permute-done | bytes 131104 | tf_op jit(solution)/shard_map/ppermute | solution.py:192
  182.8 1.0 collective-permute-done.11.b3
  183.8 0.0 collective-permute-done.9.b1
  183.8 0.8 shard_map.103
  (1 shorter events, 0.0 us)
Async XLA Ops:
  6.5 54.5 %copy-start.8 = (bf16[2,256,256]{2,1,0:T(8,128)(2,1)S(1)}, bf16[2,256,256]{2,1,0:T(8,128)(2,1)}, u32[]{:S(2)}) copy-start(bf16[2,256,256]{2,1,0:T(8,128)(2,1)} %constant.57.clone.z_ref) | copy-start | bytes 786436
  6.5 54.5 %copy-start.9 = (bf16[2,256,256]{2,1,0:T(8,128)(2,1)S(1)}, bf16[2,256,256]{2,1,0:T(8,128)(2,1)}, u32[]{:S(2)}) copy-start(bf16[2,256,256]{2,1,0:T(8,128)(2,1)} %constant.58.clone.y_ref) | copy-start | bytes 786436
  6.5 54.5 %all-gather.3.cloned.1.call-start = ((), (), s32[]{:S(2)}) async-start(), calls=%async_computation.2 | async-start | bytes 2621440 | tf_op jit(solution)/shard_map/all_gather | solution.py:213
  6.5 13.6 %collective-permute-start.3 = (f32[1,2,128,128]{3,2,1,0:T(8,128)}, f32[1,2,128,128]{3,2,1,0:T(8,128)S(1)}, u32[]{:S(2)}, u32[]{:S(2)}) collective-permute-start(f32[1,2,128,128]{3,2,1,0:T(8,128)} %param.11), channel_id=1, source_target_pairs={{0,4},{1,5},{2,6},{3,7},{4,0},{5,1},{6,2},{7,3},{8,12},{9,13},{10,... | collective-permute-start | bytes 393224 | tf_op jit(solution)/shard_map/ppermute | solution.py:192
  9.5 10.6 %collective-permute-start.4 = (f32[1,2,128,128]{3,2,1,0:T(8,128)}, f32[1,2,128,128]{3,2,1,0:T(8,128)S(1)}, u32[]{:S(2)}, u32[]{:S(2)}) collective-permute-start(f32[1,2,128,128]{3,2,1,0:T(8,128)} %param.11), channel_id=1, source_target_pairs={{0,8},{1,9},{2,10},{3,11},{4,12},{5,13},{6,14},{7,15},{8,0},{9,1},... | collective-permute-start | bytes 393224 | tf_op jit(solution)/shard_map/ppermute | solution.py:192
  13.7 12.0 %collective-permute-start.5 = (f32[1,2,128,128]{3,2,1,0:T(8,128)}, f32[1,2,128,128]{3,2,1,0:T(8,128)S(1)}, u32[]{:S(2)}, u32[]{:S(2)}) collective-permute-start(f32[1,2,128,128]{3,2,1,0:T(8,128)} %param.11), channel_id=1, source_target_pairs={{0,12},{1,13},{2,14},{3,15},{4,8},{5,9},{6,10},{7,11},{8,4},{9,5},... | collective-permute-start | bytes 393224 | tf_op jit(solution)/shard_map/ppermute | solution.py:192
  28.7 5.7 %collective-permute-start = (f32[2,128,128]{2,1,0:T(8,128)S(1)}, f32[2,128,128]{2,1,0:T(8,128)S(1)}, u32[]{:S(2)}, u32[]{:S(2)}) collective-permute-start(f32[2,128,128]{2,1,0:T(8,128)S(1)} %get-tuple-element.14), channel_id=1, source_target_pairs={{0,4},{1,5},{2,6},{3,7},{4,0},{5,1},{6,2},{7,3},{8,12},{9,13},{10,... | collective-permute-start | bytes 393224 | tf_op jit(solution)/shard_map/ppermute | solution.py:192
  29.5 9.4 %collective-permute-start.1 = (f32[2,128,128]{2,1,0:T(8,128)S(1)}, f32[2,128,128]{2,1,0:T(8,128)S(1)}, u32[]{:S(2)}, u32[]{:S(2)}) collective-permute-start(f32[2,128,128]{2,1,0:T(8,128)S(1)} %get-tuple-element.16), channel_id=1, source_target_pairs={{0,8},{1,9},{2,10},{3,11},{4,12},{5,13},{6,14},{7,15},{8,0},{9,1},... | collective-permute-start | bytes 393224 | tf_op jit(solution)/shard_map/ppermute | solution.py:192
  33.6 13.9 %collective-permute-start.2 = (f32[2,128,128]{2,1,0:T(8,128)S(1)}, f32[2,128,128]{2,1,0:T(8,128)S(1)}, u32[]{:S(2)}, u32[]{:S(2)}) collective-permute-start(f32[2,128,128]{2,1,0:T(8,128)S(1)} %get-tuple-element.13), channel_id=1, source_target_pairs={{0,12},{1,13},{2,14},{3,15},{4,8},{5,9},{6,10},{7,11},{8,4},{9,5},... | collective-permute-start | bytes 393224 | tf_op jit(solution)/shard_map/ppermute | solution.py:192
  61.1 1.6 copy-start
  65.7 1.3 copy-start.2
  67.0 7.5 %copy-start.10 = (f32[128,2,128]{2,1,0:T(2,128)S(1)}, f32[128,2,128]{2,1,0:T(2,128)}, u32[]{:S(2)}) copy-start(f32[128,2,128]{2,1,0:T(2,128)} %c0.1) | copy-start | bytes 393220
  67.0 46.9 %copy-start.6 = (bf16[2,256,256]{2,1,0:T(8,128)(2,1)S(1)}, bf16[2,256,256]{2,1,0:T(8,128)(2,1)}, u32[]{:S(2)}) copy-start(bf16[2,256,256]{2,1,0:T(8,128)(2,1)} %constant.59.clone.x_ref) | copy-start | bytes 786436
  67.0 46.9 %copy-start.7 = (bf16[2,256,256]{2,1,0:T(8,128)(2,1)S(1)}, bf16[2,256,256]{2,1,0:T(8,128)(2,1)}, u32[]{:S(2)}) copy-start(bf16[2,256,256]{2,1,0:T(8,128)(2,1)} %constant.60.clone.back_ref) | copy-start | bytes 786436
  67.0 46.9 %all-to-all-start = ((f32[16,256,128]{2,1,0:T(8,128)}), f32[16,256,128]{2,1,0:T(8,128)S(1)}, u32[]{:S(2)}, u32[]{:S(2)}) async-start(f32[16,256,128]{2,1,0:T(8,128)} %bitcast.17), calls=%async_computation | async-start | bytes 4194304 | tf_op jit(solution)/shard_map/all_to_all | solution.py:196
  74.5 37.7 %collective-permute-start.6 = (f32[128,2,128]{2,1,0:T(2,128)S(1)}, f32[128,2,128]{2,1,0:T(2,128)S(1)}, u32[]{:S(2)}, u32[]{:S(2)}) collective-permute-start(f32[128,2,128]{2,1,0:T(2,128)S(1)} %copy-done.10), channel_id=1, source_target_pairs={{0,4},{1,5},{2,6},{3,7},{4,0},{5,1},{6,2},{7,3},{8,12},{9,13},{10,... | collective-permute-start | bytes 393224 | tf_op jit(solution)/shard_map/ppermute | solution.py:192
  76.8 37.0 %collective-permute-start.7 = (f32[128,2,128]{2,1,0:T(2,128)S(1)}, f32[128,2,128]{2,1,0:T(2,128)S(1)}, u32[]{:S(2)}, u32[]{:S(2)}) collective-permute-start(f32[128,2,128]{2,1,0:T(2,128)S(1)} %copy-done.10), channel_id=1, source_target_pairs={{0,8},{1,9},{2,10},{3,11},{4,12},{5,13},{6,14},{7,15},{8,0},{9,1},... | collective-permute-start | bytes 393224 | tf_op jit(solution)/shard_map/ppermute | solution.py:192
  79.6 34.3 %collective-permute-start.8 = (f32[128,2,128]{2,1,0:T(2,128)S(1)}, f32[128,2,128]{2,1,0:T(2,128)S(1)}, u32[]{:S(2)}, u32[]{:S(2)}) collective-permute-start(f32[128,2,128]{2,1,0:T(2,128)S(1)} %copy-done.10), channel_id=1, source_target_pairs={{0,12},{1,13},{2,14},{3,15},{4,8},{5,9},{6,10},{7,11},{8,4},{9,5},... | collective-permute-start | bytes 393224 | tf_op jit(solution)/shard_map/ppermute | solution.py:192
  116.6 1.4 copy-start.3
  118.0 12.6 %copy-start.11 = (s32[4,4]{1,0:T(4,128)S(1)}, s32[4,4]{1,0:T(4,128)}, u32[]{:S(2)}) copy-start(s32[4,4]{1,0:T(4,128)} %param.13) | copy-start | bytes 196
  118.0 46.7 %copy-start.1 = (f32[16,2,128,128]{3,2,1,0:T(8,128)S(1)}, f32[16,2,128,128]{3,2,1,0:T(8,128)}, u32[]{:S(2)}) copy-start(f32[16,2,128,128]{3,2,1,0:T(8,128)} %all-gather.3.cloned.1.call-done) | copy-start | bytes 6291460
  118.0 46.7 %copy-start.4 = (bf16[2,256,256]{2,1,0:T(8,128)(2,1)S(1)}, bf16[2,256,256]{2,1,0:T(8,128)(2,1)}, u32[]{:S(2)}) copy-start(bf16[2,256,256]{2,1,0:T(8,128)(2,1)} %constant.61.clone.y_ref) | copy-start | bytes 786436
  118.0 46.7 %copy-start.5 = (bf16[2,256,256]{2,1,0:T(8,128)(2,1)S(1)}, bf16[2,256,256]{2,1,0:T(8,128)(2,1)}, u32[]{:S(2)}) copy-start(bf16[2,256,256]{2,1,0:T(8,128)(2,1)} %constant.62.clone.z_ref) | copy-start | bytes 786436
  118.0 46.7 %all-to-all-start.1 = ((f32[16,256,128]{2,1,0:T(8,128)}), f32[16,256,128]{2,1,0:T(8,128)}, u32[]{:S(2)}, u32[]{:S(2)}) async-start(f32[16,256,128]{2,1,0:T(8,128)} %bitcast.18), calls=%async_computation.1 | async-start | bytes 4194304 | tf_op jit(solution)/shard_map/all_to_all | solution.py:196
  169.0 13.8 %collective-permute-start.10 = (f32[2,128,128]{2,1,0:T(8,128)S(1)}, f32[2,128,128]{2,1,0:T(8,128)S(1)}, u32[]{:S(2)}, u32[]{:S(2)}) collective-permute-start(f32[2,128,128]{2,1,0:T(8,128)S(1)} %get-tuple-element.11), channel_id=1, source_target_pairs={{0,8},{1,9},{2,10},{3,11},{4,12},{5,13},{6,14},{7,15},{8,0},{9,1},... | collective-permute-start | bytes 393224 | tf_op jit(solution)/shard_map/ppermute | solution.py:192
  170.4 13.4 %collective-permute-start.11 = (f32[2,128,128]{2,1,0:T(8,128)S(1)}, f32[2,128,128]{2,1,0:T(8,128)S(1)}, u32[]{:S(2)}, u32[]{:S(2)}) collective-permute-start(f32[2,128,128]{2,1,0:T(8,128)S(1)} %get-tuple-element.12), channel_id=1, source_target_pairs={{0,12},{1,13},{2,14},{3,15},{4,8},{5,9},{6,10},{7,11},{8,4},{9,5},... | collective-permute-start | bytes 393224 | tf_op jit(solution)/shard_map/ppermute | solution.py:192
  171.9 11.9 %collective-permute-start.9 = (f32[2,128,128]{2,1,0:T(8,128)S(1)}, f32[2,128,128]{2,1,0:T(8,128)S(1)}, u32[]{:S(2)}, u32[]{:S(2)}) collective-permute-start(f32[2,128,128]{2,1,0:T(8,128)S(1)} %get-tuple-element.10), channel_id=1, source_target_pairs={{0,4},{1,5},{2,6},{3,7},{4,0},{5,1},{6,2},{7,3},{8,12},{9,13},{10,... | collective-permute-start | bytes 393224 | tf_op jit(solution)/shard_map/ppermute | solution.py:192
Sparse Core Ops, SparseCore 0:
  27.6 33.3 all-gather.2
